TPU v7x, 32 devices: a whole 2x2x4 slice. The times are simulated.
32 devices in a mesh: dp: 4 (over y, x), fsdp: 8 (over z, core).
Axes of the slice: x: 2, y: 2, z: 4, core: 2. Of those that a mesh axis runs over, the one named last changes fastest.
Arguments:
- x_src: bfloat16 [256, 8192], P('fsdp', 'dp'), may hold values from -6 to 6
- doc_lengths: int32 [8, 4], replicated, may hold values from 1 to 16, as said below
- doc_dests: int32 [8, 4], replicated, may hold values from 0 to 7, as said below
- w_gate: bfloat16 [8192, 14336], P('dp', 'fsdp'), may hold values from -0.0625 to 0.0625
- w_up: bfloat16 [8192, 14336], P('dp', 'fsdp'), may hold values from -0.0625 to 0.0625
- w_down: bfloat16 [14336, 8192], P('fsdp', 'dp'), may hold values from -0.046875 to 0.046875
- basis: float32 [8192, 512], P('dp'), may hold values from -0.0625 to 0.0625
- out_cotangent: bfloat16 [512, 8192], P('fsdp', 'dp'), may hold values from -6 to 6
Outputs:
- layer_out: bfloat16 [512, 8192], P('fsdp', 'dp')
- input_grad: bfloat16 [512, 8192], P('fsdp', 'dp')
- grad_gate: float32 [8192, 14336], P('dp', 'fsdp')
- grad_up: float32 [8192, 14336], P('dp', 'fsdp')
- grad_down: float32 [14336, 8192], P('fsdp', 'dp')
Inputs may be any that keep to these rules, and one draw needn't show every extreme that they name: `doc_lengths`: the 4 lengths of a source sum to 32 and one of them equals 16. `doc_dests`: document c of every source s goes to destination (s + o_c) modulo 8, for 4 different offsets o_c shared by all sources, one of which is 4; a destination receives at most 64 tokens in all, and some destination receives exactly 64.
All inputs are finite; a program needn't handle non-finite values.
Results may differ from a plain program's by a relative error of at most 0.034.
Values may be sent and summed in bfloat16 or wider, within the bound.
A program may use at most 192 MiB of HBM per device.

v0:
```python
import jax
import jax.numpy as jnp
from jax import lax
from jax.sharding import PartitionSpec as P

MOST = 16


def deal_tables(doc_lengths, doc_dests):
    groups = doc_lengths.shape[0]
    starts = jnp.cumsum(doc_lengths, axis=1) - doc_lengths
    targets = jnp.arange(groups, dtype=jnp.int32)
    hits = (doc_dests[:, :, None] == targets[None, None, :]).astype(jnp.int32)
    loads = jnp.sum(doc_lengths[:, :, None] * hits, axis=1)
    firsts = jnp.sum(starts[:, :, None] * hits, axis=1)
    return (loads, firsts)


def settle(term):
    return lax.optimization_barrier(term.astype(jnp.bfloat16)).astype(jnp.float32)


def pack_slots(rows, loads_out, firsts_out, depth):
    inner = jnp.arange(depth, dtype=jnp.int32)
    valid = inner[None, :] < loads_out[:, None]
    index = jnp.where(valid, firsts_out[:, None] + inner[None, :], 0).reshape(-1)
    taken = jnp.take(rows, index, axis=0).reshape(loads_out.shape[0], depth, rows.shape[1])
    return jnp.where(valid[:, :, None], taken, jnp.zeros_like(taken))


def compact_rows(slots, loads_in, count):
    sources, depth = (slots.shape[0], slots.shape[1])
    offsets = jnp.cumsum(loads_in) - loads_in
    ends = offsets + loads_in
    place = jnp.arange(count, dtype=jnp.int32)
    owner = jnp.sum((ends[:, None] <= place[None, :]).astype(jnp.int32), axis=0)
    owner = jnp.minimum(owner, sources - 1)
    inner = place - jnp.take(offsets, owner)
    valid = place < jnp.sum(loads_in)
    flat = jnp.where(valid, owner * depth + inner, 0)
    taken = jnp.take(slots.reshape(sources * depth, slots.shape[2]), flat, axis=0)
    return jnp.where(valid[:, None], taken, jnp.zeros_like(taken))


def layer(x_rows, dy_rows, w_gate, w_up, w_down, basis):
    hidden_width = w_gate.shape[1]
    high = lax.Precision.HIGHEST
    xall = lax.all_gather(x_rows, "fsdp", axis=0, tiled=True)
    block = xall
    first = settle(jnp.dot(block, w_gate, preferred_element_type=jnp.float32))
    second = settle(jnp.dot(block, w_up, preferred_element_type=jnp.float32))
    both = lax.psum_scatter(
        jnp.concatenate([first, second], axis=1).astype(jnp.bfloat16),
        "dp",
        scatter_dimension=0,
        tiled=True,
    ).astype(jnp.float32)
    gate = both[:, :hidden_width]
    up = both[:, hidden_width:]
    sig = jax.nn.sigmoid(gate)
    hidden = (gate * sig * up).astype(jnp.bfloat16)
    hall = lax.all_gather(hidden, "dp", axis=0, tiled=True)
    block = hall
    layer_out = lax.psum_scatter(
        settle(jnp.dot(block, w_down, preferred_element_type=jnp.float32)).astype(jnp.bfloat16),
        "fsdp",
        scatter_dimension=0,
        tiled=True,
    )
    dyall = lax.all_gather(dy_rows, "fsdp", axis=0, tiled=True)
    block = dyall
    hidden_grad = lax.psum_scatter(
        settle(
            lax.dot_general(
                block, w_down, (((1,), (1,)), ((), ())), preferred_element_type=jnp.float32
            )
        ).astype(jnp.bfloat16),
        "dp",
        scatter_dimension=0,
        tiled=True,
    ).astype(jnp.float32)
    gate_grad = (hidden_grad * up * sig * (1.0 + gate * (1.0 - sig))).astype(jnp.bfloat16)
    up_grad = (hidden_grad * gate * sig).astype(jnp.bfloat16)
    gate_all, up_all = (
        lax.all_gather(gate_grad, "dp", axis=0, tiled=True),
        lax.all_gather(up_grad, "dp", axis=0, tiled=True),
    )
    contract_rows = (((0,), (0,)), ((), ()))
    grad_down = lax.dot_general(hall, dyall, contract_rows, preferred_element_type=jnp.float32)
    raw_gate = lax.dot_general(xall, gate_all, contract_rows, preferred_element_type=jnp.float32)
    raw_up = lax.dot_general(xall, up_all, contract_rows, preferred_element_type=jnp.float32)
    first = gate_all
    second = up_all
    total = lax.dot_general(
        first, w_gate, (((1,), (1,)), ((), ())), preferred_element_type=jnp.float32
    )
    total = total + lax.dot_general(
        second, w_up, (((1,), (1,)), ((), ())), preferred_element_type=jnp.float32
    )
    input_grad = lax.psum_scatter(
        settle(total).astype(jnp.bfloat16), "fsdp", scatter_dimension=0, tiled=True
    )
    local_gate = lax.dot_general(basis, raw_gate, contract_rows, precision=high)
    local_up = lax.dot_general(basis, raw_up, contract_rows, precision=high)
    over_gate, over_up = (
        lax.psum(local_gate.astype(jnp.bfloat16), "dp").astype(jnp.float32),
        lax.psum(local_up.astype(jnp.bfloat16), "dp").astype(jnp.float32),
    )
    grad_gate = raw_gate - jnp.dot(basis, over_gate, precision=high)
    grad_up = raw_up - jnp.dot(basis, over_up, precision=high)
    return (layer_out, input_grad, grad_gate, grad_up, grad_down)


def per_device(x_src, doc_lengths, doc_dests, w_gate, w_up, w_down, basis, out_cotangent):
    loads, firsts = deal_tables(doc_lengths, doc_dests)
    myself = lax.axis_index("fsdp")
    loads_out = jnp.take(loads, myself, axis=0)
    firsts_out = jnp.take(firsts, myself, axis=0)
    loads_in = jnp.take(loads, myself, axis=1)
    dealt_rows = out_cotangent.shape[0]
    slots = pack_slots(x_src, loads_out, firsts_out, MOST)
    arrived = lax.all_to_all(slots, "fsdp", split_axis=0, concat_axis=0, tiled=True)
    x_rows = compact_rows(arrived, loads_in, dealt_rows)
    layer_out, input_grad, grad_gate, grad_up, grad_down = layer(
        x_rows, out_cotangent, w_gate, w_up, w_down, basis
    )
    return (layer_out, input_grad, grad_gate, grad_up, grad_down)


def solution(mesh):
    return jax.shard_map(
        per_device,
        mesh=mesh,
        in_specs=(
            P("fsdp", "dp"),
            P(),
            P(),
            P("dp", "fsdp"),
            P("dp", "fsdp"),
            P("fsdp", "dp"),
            P("dp", None),
            P("fsdp", "dp"),
        ),
        out_specs=(
            P("fsdp", "dp"),
            P("fsdp", "dp"),
            P("dp", "fsdp"),
            P("dp", "fsdp"),
            P("fsdp", "dp"),
        ),
        check_vma=False,
    )
```

profile of v0, /device:TPU:0, one launch (start us, length us, event | category | flops | bytes accessed | tf_op | source)
XLA Modules:
  0.0 496.8 jit_solution(12139789651017788143)
XLA Ops:
  7.2 0.7 reduce_window_sum.18
  7.9 0.7 sub.31
  8.6 0.8 select_reduce_fusion.1
  9.4 0.1 add_select_fusion
  9.5 0.1 iota_compare_fusion.1
  9.6 0.1 select_n.154
  9.7 0.9 gather_fusion
  10.6 0.9 select_select_fusion
  11.6 6.3 %all-to-all-start = ((bf16[8,16,2048]{2,1,0:T(8,128)(2,1)}), bf16[8,16,2048]{2,1,0:T(8,128)(2,1)S(1)}, u32[]{:S(2)}, u32[]{:S(2)}) async-start(bf16[8,16,2048]{2,1,0:T(8,128)(2,1)} %select_select_fusion), calls=%async_computation | async-start | bytes 1048576 | tf_op jit(solution)/shard_map/all_to_all | solution.py:122
  17.9 0.7 fusion.15
  18.7 0.1 reduce.2
  18.8 0.7 fusion.16
  19.4 0.1 convert_reduce_fusion
  19.5 5.6 %compare_and_fusion.1 = (pred[64]{0:T(512)(128)(4,1)S(1)}, s32[64]{0:T(128)S(1)}, pred[64]{0:T(512)(128)(4,1)S(1)}) fusion(s32[64]{0:T(128)S(1)} %convert_reduce_fusion, s32[]{:T(128)} %get-tuple-element.28, s32[]{:T(128)} %bitcast.9, s32[]{:T(128)} %bitcast.8, s32[]{:T(128)} %bitcast.7, s32[]{:T(128)} %bitcast.6, s32[]{:T(128)} %bitcast.5, s32[]{:T(128)} %bitcast.4, ...), kind=kLoop, calls=%fused_computation.51 | loop fusion | flops 2304 | bytes 676 | tf_op jit(solution)/shard_map/jit(_take)/and | solution.py:41
  25.1 0.7 fusion.14
  25.8 7.4 %all-to-all-done = bf16[8,16,2048]{2,1,0:T(8,128)(2,1)S(1)} async-done(((bf16[8,16,2048]{2,1,0:T(8,128)(2,1)}), bf16[8,16,2048]{2,1,0:T(8,128)(2,1)S(1)}, u32[]{:S(2)}, u32[]{:S(2)}) %all-to-all-start) | async-done | bytes 524320 | tf_op jit(solution)/shard_map/all_to_all | solution.py:122
  33.2 0.7 gather_fusion.1
  34.0 0.8 select_select_fusion.1
  34.9 0.7 all-gather.10.cloned.1.call-update
  35.6 27.4 %all-gather.6.cloned.1.call-done = bf16[512,2048]{1,0:T(8,128)(2,1)} async-done(((bf16[64,2048]{1,0:T(8,128)(2,1)}), bf16[512,2048]{1,0:T(8,128)(2,1)}) %all-gather.6.cloned.1.call-update) | async-done | bytes 2097168 | tf_op jit(solution)/shard_map/all_gather | solution.py:48
  63.0 7.8 %convolution_convert_fusion.2 = bf16[512,1792]{1,0:T(8,128)(2,1)S(1)} fusion(bf16[512,2048]{1,0:T(8,128)(2,1)} %all-gather.6.cloned.1.call-done, bf16[2048,1792]{1,0:T(8,128)(2,1)} %param.14), kind=kOutput, calls=%fused_computation.8 | convolution fusion | flops 3759013888 | bytes 11272192 | tf_op jit(solution)/shard_map/dot_general | solution.py:51
  70.8 7.3 %convolution_convert_fusion.3 = bf16[512,1792]{1,0:T(8,128)(2,1)S(1)} fusion(bf16[512,2048]{1,0:T(8,128)(2,1)S(1)} %copy-done.7, bf16[2048,1792]{1,0:T(8,128)(2,1)} %param.13), kind=kOutput, calls=%fused_computation.9 | convolution fusion | flops 3759013888 | bytes 11272192 | tf_op jit(solution)/shard_map/dot_general | solution.py:50
  78.1 2.1 pad_maximum_fusion
  80.3 13.0 %all-gather.10.cloned.1.call-done = bf16[512,2048]{1,0:T(8,128)(2,1)} async-done(((bf16[64,2048]{1,0:T(8,128)(2,1)}), bf16[512,2048]{1,0:T(8,128)(2,1)}) %all-gather.10.cloned.1.call-update) | async-done | bytes 2097168 | tf_op jit(solution)/shard_map/all_gather | solution.py:70
  93.2 8.9 %convolution_convert_fusion = bf16[512,1792]{1,0:T(8,128)(2,1)} fusion(bf16[512,2048]{1,0:T(8,128)(2,1)} %all-gather.10.cloned.1.call-done, bf16[1792,2048]{1,0:T(8,128)(2,1)} %param.15), kind=kOutput, calls=%fused_computation.6 | convolution fusion | flops 3759013888 | bytes 11272192 | tf_op jit(solution)/shard_map/dot_general | solution.py:74
  102.2 0.3 all-gather.12.cloned.1.call-start
  102.4 42.2 %reduce-scatter.5.cloned.1.call-done = bf16[128,3584]{1,0:T(8,128)(2,1)} async-done(((bf16[512,3584]{1,0:T(8,128)(2,1)}), bf16[128,3584]{1,0:T(8,128)(2,1)}) %reduce-scatter.5.cloned.1.call-update) | async-done | bytes 917520 | tf_op jit(solution)/shard_map/reduce_scatter | solution.py:52
  144.6 1.4 convert_element_type.60
  146.0 35.1 %reduce-scatter.9.cloned.1.call-done = bf16[128,1792]{1,0:T(8,128)(2,1)} async-done(((bf16[512,1792]{1,0:T(8,128)(2,1)}), bf16[128,1792]{1,0:T(8,128)(2,1)}) %reduce-scatter.9.cloned.1.call-update) | async-done | bytes 458768 | tf_op jit(solution)/shard_map/reduce_scatter | solution.py:72
  181.2 2.6 fusion.6
  183.8 0.5 all-gather.14.cloned.1.call-update
  184.4 0.7 all-gather.8.cloned.1.call-update
  185.1 31.9 %all-gather.12.cloned.1.call-done = bf16[512,1792]{1,0:T(8,128)(2,1)} async-done(((bf16[128,1792]{1,0:T(8,128)(2,1)}), bf16[512,1792]{1,0:T(8,128)(2,1)}) %all-gather.12.cloned.1.call-update) | async-done | bytes 1835024 | tf_op jit(solution)/shard_map/all_gather | solution.py:85
  217.0 11.6 %fusion.18 = f32[2048,1792]{1,0:T(8,128)} fusion(bf16[512,2048]{1,0:T(8,128)(2,1)} %all-gather.6.cloned.1.call-done, bf16[512,1792]{1,0:T(8,128)(2,1)} %all-gather.12.cloned.1.call-done), kind=kOutput, calls=%fused_computation.71 | convolution fusion | flops 3758096384 | bytes 18612224 | tf_op jit(solution)/shard_map/dot_general | solution.py:90
  228.6 23.8 %all-gather.14.cloned.1.call-done = bf16[512,1792]{1,0:T(8,128)(2,1)} async-done(((bf16[128,1792]{1,0:T(8,128)(2,1)}), bf16[512,1792]{1,0:T(8,128)(2,1)}) %all-gather.14.cloned.1.call-update) | async-done | bytes 1835024 | tf_op jit(solution)/shard_map/all_gather | solution.py:86
  252.5 11.1 %fusion.19 = f32[2048,1792]{1,0:T(8,128)} fusion(bf16[512,2048]{1,0:T(8,128)(2,1)S(1)} %copy-done.8, bf16[512,1792]{1,0:T(8,128)(2,1)} %all-gather.14.cloned.1.call-done), kind=kOutput, calls=%fused_computation.72 | convolution fusion | flops 3758096384 | bytes 18612224 | tf_op jit(solution)/shard_map/dot_general | solution.py:91
  263.5 1.0 copy-done.3
  264.5 24.8 %fusion = bf16[512,1792]{0,1:T(8,128)(2,1)} fusion(f32[2048,1792]{1,0:T(8,128)S(1)} %copy-done.2, f32[2048,512]{1,0:T(8,128)S(1)} %copy-done.3), kind=kOutput, calls=%fused_computation.12 | convolution fusion | flops 22549495808 | bytes 20709376 | tf_op jit(solution)/shard_map/dot_general | solution.py:103
  289.3 27.6 %fusion.1 = bf16[512,1792]{0,1:T(8,128)(2,1)} fusion(f32[2048,1792]{1,0:T(8,128)} %fusion.19, f32[2048,512]{1,0:T(8,128)S(1)} %copy-done.3), kind=kOutput, calls=%fused_computation.13 | convolution fusion | flops 22549495808 | bytes 20709376 | tf_op jit(solution)/shard_map/dot_general | solution.py:104
  317.1 9.0 %convolution_convert_fusion.1 = bf16[512,2048]{1,0:T(8,128)(2,1)} fusion(bf16[512,1792]{1,0:T(8,128)(2,1)} %all-gather.8.cloned.1.call-done, bf16[1792,2048]{1,0:T(8,128)(2,1)} %param.15), kind=kOutput, calls=%fused_computation.7 | convolution fusion | flops 3759144960 | bytes 11272192 | tf_op jit(solution)/shard_map/dot_general | solution.py:65
  326.2 6.4 %fusion.17 = f32[512,2048]{1,0:T(8,128)S(1)} fusion(bf16[512,1792]{1,0:T(8,128)(2,1)S(1)} %copy-done.9, bf16[2048,1792]{1,0:T(8,128)(2,1)} %param.13), kind=kOutput, calls=%fused_computation.70 | convolution fusion | flops 3758096384 | bytes 13369344 | tf_op jit(solution)/shard_map/dot_general | solution.py:94
  332.6 8.5 %add_convert_fusion = bf16[512,2048]{1,0:T(8,128)(2,1)} fusion(f32[512,2048]{1,0:T(8,128)S(1)} %fusion.17, bf16[512,1792]{1,0:T(8,128)(2,1)S(1)} %copy-done.10, bf16[2048,1792]{1,0:T(8,128)(2,1)} %param.14), kind=kOutput, calls=%fused_computation.4 | convolution fusion | flops 3760193536 | bytes 15466496 | tf_op jit(solution)/shard_map/dot_general | solution.py:97
  341.1 9.1 %fusion.20 = f32[1792,2048]{1,0:T(8,128)} fusion(bf16[512,1792]{1,0:T(8,128)(2,1)} %all-gather.8.cloned.1.call-done, bf16[512,2048]{1,0:T(8,128)(2,1)S(1)} %copy-done.6), kind=kOutput, calls=%fused_computation.73 | convolution fusion | flops 3758096384 | bytes 18612224 | tf_op jit(solution)/shard_map/dot_general | solution.py:89
  350.2 63.1 %all-reduce.3.cloned.1.call-done = (bf16[512,1792]{0,1:T(8,128)(2,1)}, bf16[512,1792]{0,1:T(8,128)(2,1)}) async-done(((bf16[512,1792]{0,1:T(8,128)(2,1)}, bf16[512,1792]{0,1:T(8,128)(2,1)}), (bf16[512,1792]{0,1:T(8,128)(2,1)}, bf16[512,1792]{0,1:T(8,128)(2,1)})) %all-reduce.3.cloned.1.call-update) | async-done | bytes 3670032 | tf_op jit(solution)/shard_map/psum | solution.py:106
  413.3 19.5 %bitcast_subtract_fusion.1 = f32[2048,1792]{1,0:T(8,128)} fusion(f32[2048,1792]{1,0:T(8,128)} %fusion.18, bf16[512,1792]{0,1:T(8,128)(2,1)} %get-tuple-element.32, f32[2048,512]{1,0:T(8,128)} %param.16), kind=kOutput, calls=%fused_computation.3 | convolution fusion | flops 22552248320 | bytes 35389440 | tf_op jit(solution)/shard_map/dot_general | solution.py:109
  432.8 17.2 %bitcast_subtract_fusion = f32[2048,1792]{1,0:T(8,128)} fusion(f32[2048,1792]{1,0:T(8,128)} %fusion.19, bf16[512,1792]{0,1:T(8,128)(2,1)S(1)} %copy-done.5, f32[2048,512]{1,0:T(8,128)S(1)} %copy-done.4), kind=kOutput, calls=%fused_computation.2 | convolution fusion | flops 22552248320 | bytes 35389440 | tf_op jit(solution)/shard_map/dot_general | solution.py:110
  450.0 2.1 reduce-scatter.7.cloned.1.call-done
  452.1 37.4 %reduce-scatter.11.cloned.1.call-done = bf16[64,2048]{1,0:T(8,128)(2,1)} async-done(((bf16[512,2048]{1,0:T(8,128)(2,1)}), bf16[64,2048]{1,0:T(8,128)(2,1)}) %reduce-scatter.11.cloned.1.call-update) | async-done | bytes 262160 | tf_op jit(solution)/shard_map/reduce_scatter | solution.py:100
  (44 shorter events, 0.6 us)
Async XLA Ops:
  7.2 2.5 copy-start
  11.6 21.7 %all-to-all-start = ((bf16[8,16,2048]{2,1,0:T(8,128)(2,1)}), bf16[8,16,2048]{2,1,0:T(8,128)(2,1)S(1)}, u32[]{:S(2)}, u32[]{:S(2)}) async-start(bf16[8,16,2048]{2,1,0:T(8,128)(2,1)} %select_select_fusion), calls=%async_computation | async-start | bytes 1048576 | tf_op jit(solution)/shard_map/all_to_all | solution.py:122
  17.9 45.1 %all-gather.6.cloned.1.call-start = ((), (), s32[]{:S(2)}) async-start(), calls=%async_computation.5 | async-start | bytes 2359296 | tf_op jit(solution)/shard_map/all_gather | solution.py:48
  34.8 58.4 %all-gather.10.cloned.1.call-start = ((), (), s32[]{:S(2)}) async-start(), calls=%async_computation.9 | async-start | bytes 2359296 | tf_op jit(solution)/shard_map/all_gather | solution.py:70
  35.6 109.1 %reduce-scatter.5.cloned.1.call-start = ((), (), s32[]{:S(2)}) async-start(), calls=%async_computation.6 | async-start | bytes 4587520 | tf_op jit(solution)/shard_map/reduce_scatter | solution.py:52
  63.0 7.8 %copy-start.7 = (bf16[512,2048]{1,0:T(8,128)(2,1)S(1)}, bf16[512,2048]{1,0:T(8,128)(2,1)}, u32[]{:S(2)}) copy-start(bf16[512,2048]{1,0:T(8,128)(2,1)} %all-gather.6.cloned.1.call-done) | copy-start | bytes 6291460
  80.2 100.9 %reduce-scatter.9.cloned.1.call-start = ((), (), s32[]{:S(2)}) async-start(), calls=%async_computation.10 | async-start | bytes 2293760 | tf_op jit(solution)/shard_map/reduce_scatter | solution.py:72
  102.2 114.8 %all-gather.12.cloned.1.call-start = ((), (), s32[]{:S(2)}) async-start(), calls=%async_computation.11 | async-start | bytes 2293760 | tf_op jit(solution)/shard_map/all_gather | solution.py:85
  183.7 68.7 %all-gather.14.cloned.1.call-start = ((), (), s32[]{:S(2)}) async-start(), calls=%async_computation.12 | async-start | bytes 2293760 | tf_op jit(solution)/shard_map/all_gather | solution.py:86
  184.3 132.8 %all-gather.8.cloned.1.call-start = ((), (), s32[]{:S(2)}) async-start(), calls=%async_computation.7 | async-start | bytes 2293760 | tf_op jit(solution)/shard_map/all_gather | solution.py:62
  185.1 67.4 %copy-start.8 = (bf16[512,2048]{1,0:T(8,128)(2,1)S(1)}, bf16[512,2048]{1,0:T(8,128)(2,1)}, u32[]{:S(2)}) copy-start(bf16[512,2048]{1,0:T(8,128)(2,1)} %all-gather.6.cloned.1.call-done) | copy-start | bytes 6291460
  185.1 228.2 %all-reduce.3.cloned.1.call-start = ((), (), s32[]{:S(2)}) async-start(), calls=%async_computation.14 | async-start | bytes 7340032 | tf_op jit(solution)/shard_map/psum | solution.py:106
  252.5 11.1 %copy-start.2 = (f32[2048,1792]{1,0:T(8,128)S(1)}, f32[2048,1792]{1,0:T(8,128)}, u32[]{:S(2)}) copy-start(f32[2048,1792]{1,0:T(8,128)} %fusion.18) | copy-start | bytes 44040196
  252.5 12.1 %copy-start.3 = (f32[2048,512]{1,0:T(8,128)S(1)}, f32[2048,512]{1,0:T(8,128)}, u32[]{:S(2)}) copy-start(f32[2048,512]{1,0:T(8,128)} %param.16) | copy-start | bytes 12582916
  317.0 9.2 %copy-start.9 = (bf16[512,1792]{1,0:T(8,128)(2,1)S(1)}, bf16[512,1792]{1,0:T(8,128)(2,1)}, u32[]{:S(2)}) copy-start(bf16[512,1792]{1,0:T(8,128)(2,1)} %all-gather.12.cloned.1.call-done) | copy-start | bytes 5505028
  317.0 135.1 %reduce-scatter.7.cloned.1.call-start = ((), (), s32[]{:S(2)}) async-start(), calls=%async_computation.8 | async-start | bytes 2359296 | tf_op jit(solution)/shard_map/reduce_scatter | solution.py:64
  326.1 163.4 %reduce-scatter.11.cloned.1.call-start = ((), (), s32[]{:S(2)}) async-start(), calls=%async_computation.13 | async-start | bytes 2359296 | tf_op jit(solution)/shard_map/reduce_scatter | solution.py:100
  326.2 6.4 %copy-start.10 = (bf16[512,1792]{1,0:T(8,128)(2,1)S(1)}, bf16[512,1792]{1,0:T(8,128)(2,1)}, u32[]{:S(2)}) copy-start(bf16[512,1792]{1,0:T(8,128)(2,1)} %all-gather.14.cloned.1.call-done) | copy-start | bytes 5505028
  332.6 8.5 %copy-start.6 = (bf16[512,2048]{1,0:T(8,128)(2,1)S(1)}, bf16[512,2048]{1,0:T(8,128)(2,1)}, u32[]{:S(2)}) copy-start(bf16[512,2048]{1,0:T(8,128)(2,1)} %all-gather.10.cloned.1.call-done) | copy-start | bytes 6291460
  413.3 19.5 %copy-start.4 = (f32[2048,512]{1,0:T(8,128)S(1)}, f32[2048,512]{1,0:T(8,128)}, u32[]{:S(2)}) copy-start(f32[2048,512]{1,0:T(8,128)} %param.16) | copy-start | bytes 12582916
  413.3 19.5 %copy-start.5 = (bf16[512,1792]{0,1:T(8,128)(2,1)S(1)}, bf16[512,1792]{0,1:T(8,128)(2,1)}, u32[]{:S(2)}) copy-start(bf16[512,1792]{0,1:T(8,128)(2,1)} %get-tuple-element.33) | copy-start | bytes 5505028
  432.8 56.7 %copy-start.1 = (bf16[32,2048]{1,0:T(8,128)(2,1)S(1)}, bf16[32,2048]{1,0:T(8,128)(2,1)}, u32[]{:S(2)}) copy-start(bf16[32,2048]{1,0:T(8,128)(2,1)} %param.10) | copy-start | bytes 393220
Sparse Core Ops, SparseCore 0:
  34.9 27.9 all-gather.5
  64.6 28.5 all-gather.9
  96.8 47.8 reduce-scatter.4
  148.1 32.9 reduce-scatter.8
  183.8 33.1 all-gather.11
  219.3 33.1 all-gather.13
  254.3 33.1 all-gather.7
  317.1 96.1 all-reduce.2
  416.3 35.8 reduce-scatter.6
  454.9 34.5 reduce-scatter.10
where the time goes:
time: 505 us; the launch traced here: 497 us
  waiting for transfers between devices  285 us (56%)
  matrix products  169 us (33%)
  other arithmetic  17.3 us (3%)
  between operations  14.8 us (3%)
  starting transfers between devices  6.94 us (1%)
    psum x1, waiting for transfers between devices, layer(): lax.psum(local_gate.astype(jnp.bfloat16), 'dp').astype(jnp.float32)  63.1 us
    reduce_scatter x1, waiting for transfers between devices, layer(): lax.psum_scatter(jnp.concatenate([first, second], axis=1).astype(jnp.bflo...  42.2 us
    reduce_scatter x1, waiting for transfers between devices, layer(): lax.psum_scatter(settle(total).astype(jnp.bfloat16), 'fsdp', scatter_dime...  37.4 us
    reduce_scatter x1, waiting for transfers between devices, layer(): lax.psum_scatter(settle(lax.dot_general(block, w_down, (((1,), (1,)), (()...  35.1 us
    all_gather x1, waiting for transfers between devices, layer(): lax.all_gather(gate_grad, 'dp', axis=0, tiled=True)  31.9 us
    dot_general x1, matrix products, layer(): local_up = lax.dot_general(basis, raw_up, contract_rows, precision=high)  27.6 us
    all_gather x1, waiting for transfers between devices, layer(): xall = lax.all_gather(x_rows, 'fsdp', axis=0, tiled=True)  27.4 us
    dot_general x1, matrix products, layer(): local_gate = lax.dot_general(basis, raw_gate, contract_rows, precision=high)  24.8 us
  transfers between devices with their start and end apart: 11, of which 10 were waited for; matrix products, arithmetic and copies ran while one was open for 36% of the time, Pallas kernels for 0%

commit v1 on v0

v1 whole, which is shorter than its diff:
```python
import jax
import jax.numpy as jnp
from jax import lax
from jax.sharding import PartitionSpec as P

DP, FS = "dp", "fsdp"
F32, BF = jnp.float32, jnp.bfloat16
ROWS = (((0,), (0,)), ((), ()))
COLS = (((1,), (1,)), ((), ()))


def dot(a, b, dims=(((1,), (0,)), ((), ())), **kw):
    return lax.dot_general(a, b, dims, preferred_element_type=F32, **kw)


def places(doc_lengths, doc_dests, tokens, recv):
    groups, docs = doc_lengths.shape
    earlier = jnp.arange(docs)[:, None] < jnp.arange(docs)[None, :]
    starts = jnp.sum(doc_lengths[:, :, None] * earlier[None], axis=1)
    same = doc_dests[:, :, None, None] == doc_dests[None, None]
    before = jnp.arange(groups)[:, None] < jnp.arange(groups)[None, :]
    same = same & before[:, None, :, None]
    offsets = jnp.sum(jnp.where(same, doc_lengths[:, :, None, None], 0), axis=(0, 1))
    base = doc_dests * recv + offsets - starts
    t = jnp.arange(tokens)[None, :, None]
    inside = (t >= starts[:, None, :]) & (t < (starts + doc_lengths)[:, None, :])
    place = jnp.sum(jnp.where(inside, base[:, None, :] + t, 0), axis=2)
    return place.reshape(1, groups * tokens).astype(jnp.int32)


def gather(x, axis):
    return lax.all_gather(x, axis, axis=0, tiled=True)


def scatter(x, axis):
    return lax.psum_scatter(x, axis, scatter_dimension=0, tiled=True)


def per_device(x_src, doc_lengths, doc_dests, w_gate, w_up, w_down, basis, dy):
    groups = doc_lengths.shape[0]
    tokens, recv = x_src.shape[0], dy.shape[0]
    width = w_gate.shape[1]
    high = lax.Precision.HIGH
    place = places(doc_lengths, doc_dests, tokens, recv)
    deal = (lax.broadcasted_iota(jnp.int32, (groups * recv, groups * tokens), 0) == place).astype(BF)

    x = gather(x_src, FS)
    g = dot(x, w_gate).astype(BF)
    u = dot(x, w_up).astype(BF)
    q = dot(x.astype(F32), basis, precision=high).astype(BF)
    both = scatter(jnp.concatenate([g, u, q], axis=1), DP).astype(F32)
    gate, up, keys = both[:, :width], both[:, width : 2 * width], both[:, 2 * width :]
    sig = jax.nn.sigmoid(gate)
    hidden = (gate * sig * up).astype(BF)

    dy_all = dot(deal, gather(dy, FS), ROWS).astype(BF)
    hg = scatter(dot(dy_all, w_down, COLS).astype(BF), DP).astype(F32)
    gate_grad = (hg * up * sig * (1.0 + gate * (1.0 - sig))).astype(BF)
    up_grad = (hg * gate * sig).astype(BF)

    first = gather(jnp.concatenate([hidden, keys.astype(BF)], axis=1), DP)
    hall, kall = first[:, :width], first[:, width:]
    second = gather(jnp.concatenate([gate_grad, up_grad], axis=1), DP)
    ggall, ugall = second[:, :width], second[:, width:]

    part = dot(hall, w_down).astype(BF)
    layer_out = scatter(dot(deal, part).astype(BF), FS)
    part = (dot(ggall, w_gate, COLS) + dot(ugall, w_up, COLS)).astype(BF)
    input_grad = scatter(dot(deal, part).astype(BF), FS)

    x_proj = (x.astype(F32) - dot(kall.astype(F32), basis, COLS, precision=high)).astype(BF)
    grad_down = dot(hall, dy_all, ROWS)
    grad_gate = dot(x_proj, ggall, ROWS)
    grad_up = dot(x_proj, ugall, ROWS)
    return layer_out, input_grad, grad_gate, grad_up, grad_down


def solution(mesh):
    tiled = P(FS, DP)
    return jax.shard_map(
        per_device,
        mesh=mesh,
        in_specs=(tiled, P(), P(), P(DP, FS), P(DP, FS), tiled, P(DP, None), tiled),
        out_specs=(tiled, tiled, P(DP, FS), P(DP, FS), tiled),
        check_vma=False,
    )
```

time: 505 us -> 283 us (0.56); the launches traced: 497 us -> 283 us
  matrix products: 169 us -> 68.4 us
  waiting for transfers between devices: 285 us -> 190 us
  other arithmetic: 17.3 us -> 7.38 us
  starting transfers between devices: 6.94 us -> 0.5 us
    dot_general x13 -> x12, matrix products: 169 us -> 68.4 us  [dot(): return lax.dot_general(a, b, dims, preferred_element_type=F32, **kw)]
    psum x1 -> x0, waiting for transfers between devices: 63.1 us -> none  [layer(): lax.psum(local_gate.astype(jnp.bfloat16), 'dp').astype(jnp.float32)]
    reduce_scatter x4, waiting for transfers between devices: 117 us -> 92.7 us  [scatter(): return lax.psum_scatter(x, axis, scatter_dimension=0, tiled=True)]
    all_to_all x1 -> x0, waiting for transfers between devices: 7.45 us -> none  [per_device(): lax.all_to_all(slots, 'fsdp', split_axis=0, concat_axis=0, tiled=True)]
    all_to_all x1 -> x0, starting transfers between devices: 6.33 us -> none  [per_device(): lax.all_to_all(slots, 'fsdp', split_axis=0, concat_axis=0, tiled=True)]
    and x1 -> x0, other arithmetic: 5.59 us -> none  [compact_rows(): jnp.take(slots.reshape(sources * depth, slots.shape[2]), flat, axis=0)]
    all_gather x5 -> x4, waiting for transfers between devices: 96.1 us -> 96.1 us  [gather(): return lax.all_gather(x, axis, axis=0, tiled=True)]
  transfers between devices with their start and end apart: 11 -> 8, of which waited for: 10 -> 7; matrix products, arithmetic and copies ran while one was open for 36% -> 26% of each run, Pallas kernels for 0% -> 0%
where the time goes in v1:
time: 283 us
  waiting for transfers between devices  190 us (67%)
  matrix products  68.4 us (24%)
  between operations  14.3 us (5%)
  other arithmetic  7.38 us (3%)
    all_gather x4, waiting for transfers between devices, gather(): return lax.all_gather(x, axis, axis=0, tiled=True)  96.1 us
    reduce_scatter x4, waiting for transfers between devices, scatter(): return lax.psum_scatter(x, axis, scatter_dimension=0, tiled=True)  92.7 us
    dot_general x12, matrix products, dot(): return lax.dot_general(a, b, dims, preferred_element_type=F32, **kw)  68.4 us
  transfers between devices with their start and end apart: 8, of which 7 were waited for; matrix products, arithmetic and copies ran while one was open for 26% of the time, Pallas kernels for 0%

profile of v1, /device:TPU:0, one launch (start us, length us, event | category | flops | bytes accessed | tf_op | source)
XLA Modules:
  0.0 282.7 jit_solution(2505367204731265347)
XLA Ops:
  7.2 0.0 all-gather.5.cloned.1.call-start
  7.2 0.7 all-gather.5.cloned.1.call-update
  7.9 0.0 all-gather.9.cloned.1.call-start
  7.9 0.7 all-gather.9.cloned.1.call-update
  8.6 0.0 reduce-scatter.5.cloned.1.call-start
  8.7 25.7 %all-gather.5.cloned.1.call-done = bf16[256,2048]{1,0:T(8,128)(2,1)} async-done(((bf16[32,2048]{1,0:T(8,128)(2,1)}), bf16[256,2048]{1,0:T(8,128)(2,1)}) %all-gather.5.cloned.1.call-update) | async-done | bytes 1048592 | tf_op jit(solution)/shard_map/all_gather | solution.py:32
  34.4 4.0 %convolution_convert_fusion.7 = bf16[256,512]{1,0:T(8,128)(2,1)S(1)} fusion(bf16[256,2048]{1,0:T(8,128)(2,1)} %all-gather.5.cloned.1.call-done, f32[2048,512]{1,0:T(8,128)} %param.14), kind=kOutput, calls=%fused_computation.12 | convolution fusion | flops 1610743808 | bytes 5505024 | tf_op jit(solution)/shard_map/dot_general | solution.py:13
  38.4 0.0 copy-done
  38.4 0.0 slice-start.2
  38.4 5.3 %convolution_convert_fusion.5 = bf16[256,1792]{1,0:T(8,128)(2,1)S(1)} fusion(bf16[256,2048]{1,0:T(8,128)(2,1)S(1)} %copy-done, bf16[2048,1792]{1,0:T(8,128)(2,1)} %param.12), kind=kOutput, calls=%fused_computation.8 | convolution fusion | flops 1879506944 | bytes 9306112 | tf_op jit(solution)/shard_map/dot_general | solution.py:13
  43.8 2.1 convolution_convert_fusion.6
  45.8 1.6 pad_maximum_fusion
  47.4 0.0 reduce-scatter.5.cloned.1.call-update
  47.4 0.0 reduce-scatter.9.cloned.1.call-start
  47.5 0.6 copy-done.3
  48.1 0.1 multiply_reduce_fusion
  48.2 0.1 select_reduce_fusion
  48.3 0.1 select_reduce_fusion.1
  48.4 0.1 eq.26
  48.4 16.3 %all-gather.9.cloned.1.call-done = bf16[512,2048]{1,0:T(8,128)(2,1)} async-done(((bf16[64,2048]{1,0:T(8,128)(2,1)}), bf16[512,2048]{1,0:T(8,128)(2,1)}) %all-gather.9.cloned.1.call-update) | async-done | bytes 2097168 | tf_op jit(solution)/shard_map/all_gather | solution.py:32
  64.8 2.3 convolution_convert_fusion.3
  67.1 6.1 %convolution_convert_fusion.2 = bf16[256,1792]{1,0:T(8,128)(2,1)} fusion(bf16[256,2048]{1,0:T(8,128)(2,1)S(1)} %convolution_convert_fusion.3, bf16[1792,2048]{1,0:T(8,128)(2,1)} %param.13), kind=kOutput, calls=%fused_computation.5 | convolution fusion | flops 1879506944 | bytes 9306112 | tf_op jit(solution)/shard_map/dot_general | solution.py:13
  73.2 0.0 reduce-scatter.9.cloned.1.call-update
  73.3 0.0 all-gather.7.cloned.1.call-start
  73.3 29.7 %reduce-scatter.5.cloned.1.call-done = bf16[64,4096]{1,0:T(8,128)(2,1)} async-done(((bf16[256,4096]{1,0:T(8,128)(2,1)}), bf16[64,4096]{1,0:T(8,128)(2,1)}) %reduce-scatter.5.cloned.1.call-update) | async-done | bytes 524304 | tf_op jit(solution)/shard_map/reduce_scatter | solution.py:36
  103.0 1.2 convert_element_type.64
  104.2 29.4 %reduce-scatter.9.cloned.1.call-done = bf16[64,1792]{1,0:T(8,128)(2,1)} async-done(((bf16[256,1792]{1,0:T(8,128)(2,1)}), bf16[64,1792]{1,0:T(8,128)(2,1)}) %reduce-scatter.9.cloned.1.call-update) | async-done | bytes 229392 | tf_op jit(solution)/shard_map/reduce_scatter | solution.py:36
  133.6 1.9 fusion.16
  135.5 0.7 pad_maximum_fusion.2
  136.2 0.0 all-gather.7.cloned.1.call-update
  136.2 0.0 all-gather.11.cloned.1.call-start
  136.3 1.7 pad_maximum_fusion.1
  138.0 0.0 all-gather.11.cloned.1.call-update
  138.0 0.0 reduce-scatter.7.cloned.1.call-start
  138.1 26.0 %all-gather.7.cloned.1.call-done = bf16[256,2304]{1,0:T(8,128)(2,1)} async-done(((bf16[64,2304]{1,0:T(8,128)(2,1)}), bf16[256,2304]{1,0:T(8,128)(2,1)}) %all-gather.7.cloned.1.call-update) | async-done | bytes 1179664 | tf_op jit(solution)/shard_map/all_gather | solution.py:32
  164.1 7.3 %convolution_convert_fusion.1 = bf16[512,2048]{1,0:T(8,128)(2,1)} fusion(bf16[1792,2048]{1,0:T(8,128)(2,1)} %param.13, bf16[256,2304]{1,0:T(8,128)(2,1)} %all-gather.7.cloned.1.call-done, s32[256]{0:T(256)S(1)} %eq.26), kind=kOutput, calls=%fused_computation.1 | convolution fusion | flops 2417623040 | bytes 10355712 | tf_op jit(solution)/shard_map/dot_general | solution.py:13
  171.4 0.0 reduce-scatter.7.cloned.1.call-update
  171.5 0.2 reduce-scatter.11.cloned.1.call-start
  171.7 28.0 %all-gather.11.cloned.1.call-done = bf16[256,3584]{1,0:T(8,128)(2,1)} async-done(((bf16[64,3584]{1,0:T(8,128)(2,1)}), bf16[256,3584]{1,0:T(8,128)(2,1)}) %all-gather.11.cloned.1.call-update) | async-done | bytes 1835024 | tf_op jit(solution)/shard_map/all_gather | solution.py:32
  199.7 6.8 %fusion.8 = f32[256,2048]{1,0:T(8,128)} fusion(bf16[2048,1792]{1,0:T(8,128)(2,1)} %param.11, bf16[256,3584]{1,0:T(8,128)(2,1)} %all-gather.11.cloned.1.call-done), kind=kOutput, calls=%fused_computation.18 | convolution fusion | flops 1879048192 | bytes 10354688 | tf_op jit(solution)/shard_map/dot_general | solution.py:13
  206.5 8.1 %convolution_convert_fusion = bf16[512,2048]{1,0:T(8,128)(2,1)} fusion(f32[256,2048]{1,0:T(8,128)} %fusion.8, bf16[2048,1792]{1,0:T(8,128)(2,1)} %param.12, bf16[256,3584]{1,0:T(8,128)(2,1)} %all-gather.11.cloned.1.call-done, s32[256]{0:T(256)S(1)} %eq.26), kind=kOutput, calls=%fused_computation | convolution fusion | flops 2418147328 | bytes 12452864 | tf_op jit(solution)/shard_map/dot_general | solution.py:13
  214.6 0.0 reduce-scatter.11.cloned.1.call-update
  214.6 1.3 copy-done.2
  215.9 3.6 %fusion = bf16[256,2048]{1,0:T(8,128)(2,1)S(1)} fusion(f32[2048,512]{1,0:T(8,128)} %param.14, bf16[256,2048]{1,0:T(8,128)(2,1)S(1)} %copy-done, bf16[256,2304]{1,0:T(8,128)(2,1)S(1)} %copy-done.2), kind=kOutput, calls=%fused_computation.4 | convolution fusion | flops 1612185600 | bytes 6553600 | tf_op jit(solution)/shard_map/dot_general | solution.py:13
  219.5 7.6 %fusion.10 = f32[1792,2048]{1,0:T(8,128)} fusion(bf16[256,2048]{1,0:T(8,128)(2,1)S(1)} %convolution_convert_fusion.3, bf16[256,2304]{1,0:T(8,128)(2,1)S(1)} %copy-done.2), kind=kOutput, calls=%fused_computation.20 | convolution fusion | flops 1879048192 | bytes 16646144 | tf_op jit(solution)/shard_map/dot_general | solution.py:13
  227.1 7.6 %fusion.6 = f32[2048,1792]{1,0:T(8,128)} fusion(bf16[256,2048]{1,0:T(8,128)(2,1)S(1)} %fusion, bf16[256,3584]{1,0:T(8,128)(2,1)S(1)} %copy-done.1), kind=kOutput, calls=%fused_computation.16 | convolution fusion | flops 1879048192 | bytes 16646144 | tf_op jit(solution)/shard_map/dot_general | solution.py:13
  234.7 7.6 %fusion.2 = f32[2048,1792]{1,0:T(8,128)} fusion(bf16[256,2048]{1,0:T(8,128)(2,1)S(1)} %fusion, bf16[256,3584]{1,0:T(8,128)(2,1)S(1)} %copy-done.1), kind=kOutput, calls=%fused_computation.13 | convolution fusion | flops 1879048192 | bytes 16646144 | tf_op jit(solution)/shard_map/dot_general | solution.py:13
  242.3 33.6 %reduce-scatter.11.cloned.1.call-done = bf16[64,2048]{1,0:T(8,128)(2,1)} async-done(((bf16[512,2048]{1,0:T(8,128)(2,1)}), bf16[64,2048]{1,0:T(8,128)(2,1)}) %reduce-scatter.11.cloned.1.call-update) | async-done | bytes 262160 | tf_op jit(solution)/shard_map/reduce_scatter | solution.py:36
  (17 shorter events, 0.0 us)
Async XLA Ops:
  7.2 27.3 %all-gather.5.cloned.1.call-start = ((), (), s32[]{:S(2)}) async-start(), calls=%async_computation.4 | async-start | bytes 1179648 | tf_op jit(solution)/shard_map/all_gather | solution.py:32
  7.9 56.9 %all-gather.9.cloned.1.call-start = ((), (), s32[]{:S(2)}) async-start(), calls=%async_computation.8 | async-start | bytes 2359296 | tf_op jit(solution)/shard_map/all_gather | solution.py:32
  8.6 94.4 %reduce-scatter.5.cloned.1.call-start = ((), (), s32[]{:S(2)}) async-start(), calls=%async_computation.5 | async-start | bytes 2621440 | tf_op jit(solution)/shard_map/reduce_scatter | solution.py:36
  34.4 4.0 %copy-start = (bf16[256,2048]{1,0:T(8,128)(2,1)S(1)}, bf16[256,2048]{1,0:T(8,128)(2,1)}, u32[]{:S(2)}) copy-start(bf16[256,2048]{1,0:T(8,128)(2,1)} %all-gather.5.cloned.1.call-done) | copy-start | bytes 3145732
  34.4 9.3 %slice-start.1 = ((s8[7340032]{0:T(1024)(128)(4,1)}), s8[4194304]{0:T(1024)(128)(4,1)S(1)}, s32[]{:S(2)}) async-start(s8[7340032]{0:T(1024)(128)(4,1)} %bitcast.16), calls=%async_computation.13 | async-start | bytes 8388608
  38.4 5.3 %slice-start.2 = ((s8[7340032]{0:T(1024)(128)(4,1)}), s8[3145728]{0:T(1024)(128)(4,1)S(1)}, s32[]{:S(2)}) async-start(s8[7340032]{0:T(1024)(128)(4,1)} %bitcast.16), calls=%async_computation.14 | async-start | bytes 6291456
  47.4 0.7 copy-start.3
  47.4 0.8 copy-start.4
  47.4 86.2 %reduce-scatter.9.cloned.1.call-start = ((), (), s32[]{:S(2)}) async-start(), calls=%async_computation.9 | async-start | bytes 1146880 | tf_op jit(solution)/shard_map/reduce_scatter | solution.py:36
  73.3 90.8 %all-gather.7.cloned.1.call-start = ((), (), s32[]{:S(2)}) async-start(), calls=%async_computation.6 | async-start | bytes 1474560 | tf_op jit(solution)/shard_map/all_gather | solution.py:32
  103.0 32.4 %slice-start = ((bf16[64,4096]{1,0:T(8,128)(2,1)}), bf16[64,512]{1,0:T(8,128)(2,1)S(1)}, s32[]{:S(2)}) async-start(bf16[64,4096]{1,0:T(8,128)(2,1)} %reduce-scatter.5.cloned.1.call-done), calls=%async_computation.12 | async-start | bytes 131072 | tf_op jit(solution)/shard_map/slice | solution.py:52
  136.2 63.5 %all-gather.11.cloned.1.call-start = ((), (), s32[]{:S(2)}) async-start(), calls=%async_computation.10 | async-start | bytes 2293760 | tf_op jit(solution)/shard_map/all_gather | solution.py:32
  138.0 104.2 %reduce-scatter.7.cloned.1.call-start = ((), (), s32[]{:S(2)}) async-start(), calls=%async_computation.7 | async-start | bytes 2359296 | tf_op jit(solution)/shard_map/reduce_scatter | solution.py:36
  171.5 104.4 %reduce-scatter.11.cloned.1.call-start = ((), (), s32[]{:S(2)}) async-start(), calls=%async_computation.11 | async-start | bytes 2359296 | tf_op jit(solution)/shard_map/reduce_scatter | solution.py:36
  214.6 1.3 copy-start.2
  219.5 7.6 %copy-start.1 = (bf16[256,3584]{1,0:T(8,128)(2,1)S(1)}, bf16[256,3584]{1,0:T(8,128)(2,1)}, u32[]{:S(2)}) copy-start(bf16[256,3584]{1,0:T(8,128)(2,1)} %all-gather.11.cloned.1.call-done) | copy-start | bytes 5505028
Sparse Core Ops, SparseCore 0:
  9.6 24.7 all-gather.4
  36.0 28.7 all-gather.8
  68.3 34.6 reduce-scatter.4
  106.7 26.8 reduce-scatter.8
  136.4 27.6 all-gather.6
  166.5 33.1 all-gather.10
  202.7 35.7 reduce-scatter.6
  241.5 34.3 reduce-scatter.10
